TPU v7x, 32 devices: a whole 2x2x4 slice. The times are simulated.
32 devices in a mesh: local: 4 (over y, x), strided: 4 (over z), rep: 2 (over core).
Axes of the slice: x: 2, y: 2, z: 4, core: 2. Of those that a mesh axis runs over, the one named last changes fastest.
Arguments:
- tokens: bfloat16 [2, 512, 1440], P('rep', ('local', 'strided')), may hold values from -6 to 6
- experts: int32 [2, 512, 4], P('rep', ('local', 'strided')), may hold values from 0 to 15, as said below
- slots: int32 [2, 512, 4], P('rep', ('local', 'strided')), may hold values from -1 to 127, as said below
- route_weight: float32 [2, 512, 4], P('rep', ('local', 'strided')), may hold values from 0.05 to 0.8
- out_grad: bfloat16 [2, 512, 1440], P('rep', ('local', 'strided')), may hold values from -1.5 to 1.5
- w_gate: bfloat16 [16, 1440, 1440], P(('local', 'strided'), None, 'rep'), may hold values from -0.15625 to 0.15625
- w_up: bfloat16 [16, 1440, 1440], P(('local', 'strided'), None, 'rep'), may hold values from -0.15625 to 0.15625
- w_down: bfloat16 [16, 1440, 1440], P(('local', 'strided'), 'rep'), may hold values from -0.15625 to 0.15625
Outputs:
- mixed: bfloat16 [2, 512, 1440], P('rep', ('local', 'strided'))
- token_grad: bfloat16 [2, 512, 1440], P('rep', ('local', 'strided'))
- weight_grad: float32 [2, 512, 4], P('rep', ('local', 'strided'))
- gate_grad: bfloat16 [16, 1440, 1440], P(('local', 'strided'), None, 'rep')
- up_grad: bfloat16 [16, 1440, 1440], P(('local', 'strided'), None, 'rep')
- down_grad: bfloat16 [16, 1440, 1440], P(('local', 'strided'), 'rep')
Inputs may be any that keep to these rules, and one draw needn't show every extreme that they name: Each row names 4 different experts. The 32 rows of one device of a replica name each expert at most 16 times, and some expert exactly 16 times. slots[r, t, k] is the number of pairs of replica r that come before (t, k) in token order and name the same expert, where that number is below 128; otherwise it is -1 and the pair is dropped.
All inputs are finite; a program needn't handle non-finite values.
Results may differ from a plain program's by a relative error of at most 0.0064.
Values may be sent and summed in bfloat16 or wider, within the bound.
A program may use at most 192 MiB of HBM per device.

v0:
```python
import jax
import jax.numpy as jnp
from jax import lax
from jax.sharding import PartitionSpec as P

SWIGLU_ALPHA = 1.702


def for_sending(value):
    return jax.tree.map(lambda a: a.astype(jnp.bfloat16) if a.dtype == jnp.float32 else a, value)


def swiglu(gate_pre, up_pre):
    return (up_pre + 1.0) * gate_pre * jax.nn.sigmoid(SWIGLU_ALPHA * gate_pre)


def swiglu_grads(grad_hidden, gate_pre, up_pre):
    sigmoid_gate = jax.nn.sigmoid(SWIGLU_ALPHA * gate_pre)
    grad_up = grad_hidden * gate_pre * sigmoid_gate
    slope = sigmoid_gate + SWIGLU_ALPHA * gate_pre * sigmoid_gate * (1.0 - sigmoid_gate)
    grad_gate = grad_hidden * (up_pre + 1.0) * slope
    return (grad_gate.astype(jnp.bfloat16), grad_up.astype(jnp.bfloat16))


def contract(left, right, left_dim, right_dim):
    return lax.dot_general(
        left, right, (((left_dim,), (right_dim,)), ((), ())), preferred_element_type=jnp.float32
    )


def split_flat(values):
    return values.reshape(
        (lax.axis_size("local") * lax.axis_size("strided"), -1) + values.shape[1:]
    )


def unsplit(moved, initial):
    return tuple((item.reshape((-1,) + shaped.shape[1:]) for item, shaped in zip(moved, initial)))


def dispatch_rows(payload):
    moved = lax.all_to_all(
        for_sending(tuple((split_flat(item) for item in payload))),
        ("local", "strided"),
        split_axis=0,
        concat_axis=0,
        tiled=True,
    )
    return unsplit(moved, payload)


def return_outputs(rows):
    model_width = rows.shape[-1]
    moved = lax.all_to_all(
        split_flat(rows), ("local", "strided"), split_axis=0, concat_axis=0, tiled=True
    )
    return moved.reshape(-1, model_width)


def dispatch_grads(rows):
    model_width = rows.shape[-1]
    moved = lax.all_to_all(
        split_flat(rows), ("local", "strided"), split_axis=0, concat_axis=0, tiled=True
    )
    return moved.reshape(-1, model_width)


def return_grads(rows):
    model_width = rows.shape[-1]
    moved = lax.all_to_all(
        split_flat(rows), ("local", "strided"), split_axis=0, concat_axis=0, tiled=True
    )
    return moved.reshape(-1, model_width)


def local(tokens, experts, slots, route_weight, out_grad, w_gate, w_up, w_down):
    token_rows = tokens[0]
    token_count, model_width = token_rows.shape
    top_count = experts.shape[2]
    expert_count = lax.axis_size("local") * lax.axis_size("strided")
    capacity = token_count * top_count
    pair_most = 2 * capacity // expert_count
    buffer_rows = expert_count * pair_most
    expert_flat = experts[0].reshape(-1)
    slot_flat = slots[0].reshape(-1)
    onehot = (expert_flat[:, None] == jnp.arange(expert_count, dtype=jnp.int32)[None, :]).astype(
        jnp.int32
    )
    slot_rank = jnp.sum((jnp.cumsum(onehot, axis=0) - onehot) * onehot, axis=1)
    send_place = expert_flat * pair_most + slot_rank

    def to_buffer(pair_rows):
        return jnp.zeros((buffer_rows, model_width), pair_rows.dtype).at[send_place].set(pair_rows)

    send_slots = jnp.full((buffer_rows,), -1, jnp.int32).at[send_place].set(slot_flat)
    pair_tokens = jnp.repeat(token_rows, top_count, axis=0)
    router = route_weight[0]
    grad_rows = out_grad[0].astype(jnp.float32)
    pair_grad = (
        (router[:, :, None] * grad_rows[:, None, :]).astype(jnp.bfloat16).reshape(-1, model_width)
    )
    got_rows, got_slots = dispatch_rows((to_buffer(pair_tokens), send_slots))
    kept_mask = got_slots >= 0
    slot_target = jnp.where(kept_mask, got_slots, capacity)
    slot_source = jnp.where(kept_mask, got_slots, 0)

    def to_slots(received):
        return (
            jnp.zeros((capacity, model_width), received.dtype)
            .at[slot_target]
            .set(received, mode="drop")
        )

    def from_slots(slot_rows):
        picked = slot_rows[slot_source]
        return jnp.where(kept_mask[:, None], picked, jnp.zeros_like(picked))

    expert_rows = to_slots(got_rows)
    gate_shard = w_gate[0]
    up_shard = w_up[0]
    down_shard = w_down[0]
    gate_full, up_full, down_full = (
        lax.all_gather(gate_shard, "rep", axis=1, tiled=True),
        lax.all_gather(up_shard, "rep", axis=1, tiled=True),
        lax.all_gather(down_shard, "rep", axis=0, tiled=True),
    )
    gate_pre = contract(expert_rows, gate_full, 1, 0)
    up_pre = contract(expert_rows, up_full, 1, 0)
    hidden = swiglu(gate_pre, up_pre).astype(jnp.bfloat16)
    expert_out = contract(hidden, down_full, 1, 0).astype(jnp.bfloat16)
    pair_out = return_outputs(from_slots(expert_out))[send_place].reshape(
        token_count, top_count, model_width
    )
    mixed = jnp.sum(router[:, :, None] * pair_out.astype(jnp.float32), axis=1).astype(jnp.bfloat16)
    weight_grad = jnp.sum(grad_rows[:, None, :] * pair_out.astype(jnp.float32), axis=2)
    expert_grads = to_slots(dispatch_grads(to_buffer(pair_grad)))
    grad_hidden = contract(expert_grads, down_full, 1, 1)
    grad_gate, grad_up = swiglu_grads(grad_hidden, gate_pre, up_pre)
    rows_grad = (contract(grad_gate, gate_full, 1, 1) + contract(grad_up, up_full, 1, 1)).astype(
        jnp.bfloat16
    )
    gate_grad, up_grad, down_grad = (
        lax.psum_scatter(
            contract(expert_rows, grad_gate, 0, 0), "rep", scatter_dimension=1, tiled=True
        ),
        lax.psum_scatter(
            contract(expert_rows, grad_up, 0, 0), "rep", scatter_dimension=1, tiled=True
        ),
        lax.psum_scatter(
            contract(hidden, expert_grads, 0, 0), "rep", scatter_dimension=0, tiled=True
        ),
    )
    pair_dx = return_grads(from_slots(rows_grad))[send_place].reshape(
        token_count, top_count, model_width
    )
    token_grad = jnp.sum(pair_dx.astype(jnp.float32), axis=1).astype(jnp.bfloat16)
    return (
        mixed[None],
        token_grad[None],
        weight_grad[None],
        gate_grad.astype(jnp.bfloat16)[None],
        up_grad.astype(jnp.bfloat16)[None],
        down_grad.astype(jnp.bfloat16)[None],
    )


def solution(mesh):
    placed = (
        P("rep", ("local", "strided"), None),
        P("rep", ("local", "strided"), None),
        P("rep", ("local", "strided"), None),
        P("rep", ("local", "strided"), None),
        P("rep", ("local", "strided"), None),
        P(("local", "strided"), None, "rep"),
        P(("local", "strided"), None, "rep"),
        P(("local", "strided"), "rep", None),
    )
    return jax.shard_map(
        local,
        mesh=mesh,
        in_specs=placed,
        out_specs=(
            P("rep", ("local", "strided"), None),
            P("rep", ("local", "strided"), None),
            P("rep", ("local", "strided"), None),
            P(("local", "strided"), None, "rep"),
            P(("local", "strided"), None, "rep"),
            P(("local", "strided"), "rep", None),
        ),
        check_vma=False,
    )
```

profile of v0, /device:TPU:0, one launch (start us, length us, event | category | flops | bytes accessed | tf_op | source)
XLA Modules:
  0.0 257.3 jit_solution(1733364619276303661)
XLA Ops:
  7.2 12.3 %copy.43 = bf16[1,1440,720]{1,0,2:T(2,128)(2,1)} copy(bf16[1,1440,720]{2,1,0:T(8,128)(2,1)} %param.14) | data formatting | bytes 4147200 | tf_op args[6]
  19.6 9.2 %copy.45 = bf16[1,1440,720]{1,0,2:T(2,128)(2,1)} copy(bf16[1,1440,720]{2,1,0:T(8,128)(2,1)S(1)} %copy-done.1) | data formatting | bytes 4147200 | tf_op args[5]
  32.4 8.3 %all-to-all-start = ((s32[16,1,16]{2,1,0:T(1,128)}), s32[16,1,16]{2,1,0:T(1,128)S(1)}, u32[]{:S(2)}, u32[]{:S(2)}) async-start(s32[16,1,16]{2,1,0:T(1,128)} %all_to_all.18), calls=%async_computation | async-start | bytes 16384 | tf_op jit(solution)/shard_map/all_to_all | solution.py:42
  43.1 4.8 %all-to-all-done = s32[16,1,16]{2,1,0:T(1,128)S(1)} async-done(((s32[16,1,16]{2,1,0:T(1,128)}), s32[16,1,16]{2,1,0:T(1,128)S(1)}, u32[]{:S(2)}, u32[]{:S(2)}) %all-to-all-start) | async-done | bytes 1056 | tf_op jit(solution)/shard_map/all_to_all | solution.py:42
  47.9 3.6 %all-to-all-start.1 = ((bf16[16,16,1440]{2,1,0:T(8,128)(2,1)}), bf16[16,16,1440]{2,1,0:T(8,128)(2,1)S(1)}, u32[]{:S(2)}, u32[]{:S(2)}) async-start(bf16[16,16,1440]{2,1,0:T(8,128)(2,1)} %bitcast.7), calls=%async_computation.1 | async-start | bytes 1572864 | tf_op jit(solution)/shard_map/all_to_all | solution.py:42
  54.4 17.8 %all-to-all-done.1 = bf16[16,16,1440]{2,1,0:T(8,128)(2,1)S(1)} async-done(((bf16[16,16,1440]{2,1,0:T(8,128)(2,1)}), bf16[16,16,1440]{2,1,0:T(8,128)(2,1)S(1)}, u32[]{:S(2)}, u32[]{:S(2)}) %all-to-all-start.1) | async-done | bytes 737312 | tf_op jit(solution)/shard_map/all_to_all | solution.py:42
  72.1 3.6 %all-to-all-start.3 = ((bf16[16,16,1440]{2,1,0:T(8,128)(2,1)}), bf16[16,16,1440]{2,1,0:T(8,128)(2,1)S(1)}, u32[]{:S(2)}, u32[]{:S(2)}) async-start(bf16[16,16,1440]{2,1,0:T(8,128)(2,1)} %bitcast.17), calls=%async_computation.3 | async-start | bytes 1572864 | tf_op jit(solution)/shard_map/all_to_all | solution.py:62
  78.9 17.8 %all-to-all-done.3 = bf16[16,16,1440]{2,1,0:T(8,128)(2,1)S(1)} async-done(((bf16[16,16,1440]{2,1,0:T(8,128)(2,1)}), bf16[16,16,1440]{2,1,0:T(8,128)(2,1)S(1)}, u32[]{:S(2)}, u32[]{:S(2)}) %all-to-all-start.3) | async-done | bytes 737312 | tf_op jit(solution)/shard_map/all_to_all | solution.py:62
  98.8 22.2 %copy.44 = bf16[1,1440,1440]{2,1,0:T(8,128)(2,1)} copy(bf16[1,1440,1440]{1,0,2:T(2,128)(2,1)} %all-gather.7.cloned.1.call-done) | data formatting | bytes 8294400 | tf_op jit(solution)/shard_map/all_gather | solution.py:124
  121.0 22.3 %copy.46 = bf16[1,1440,1440]{2,1,0:T(8,128)(2,1)} copy(bf16[1,1440,1440]{1,0,2:T(2,128)(2,1)} %all-gather.9.cloned.1.call-done) | data formatting | bytes 8294400 | tf_op jit(solution)/shard_map/all_gather | solution.py:123
  143.3 4.0 %fusion.12 = f32[128,1440]{0,1:T(8,128)S(1)} fusion(bf16[128,1440]{1,0:T(8,128)(2,1)S(1)} %scatter_custom_fusion.2, bf16[1,1440,1440]{2,1,0:T(8,128)(2,1)} %copy.44), kind=kOutput, calls=%fused_computation.23 | convolution fusion | flops 531025920 | bytes 5253120 | tf_op jit(solution)/shard_map/dot_general | solution.py:26
  150.2 3.8 %multiply_convert_fusion.1 = (bf16[128,1440]{0,1:T(8,128)(2,1)S(1)}, bf16[128,1440]{0,1:T(8,128)(2,1)S(1)}, bf16[128,1440]{0,1:T(8,128)(2,1)S(1)}) fusion(f32[128,1440]{0,1:T(8,128)} %fusion.6, f32[128,1440]{0,1:T(8,128)S(1)} %fusion.12, bf16[128,1440]{1,0:T(8,128)(2,1)S(1)} %scatter_custom_fusion.4, bf16[1,1440,1440]{2,1,0:T(8,128)(2,1)} %all-gather.11.cloned.1.call-done), kind=kOutput, calls=%fused_computation.35 | convolution fusion | flops 533975040 | bytes 7096320 | tf_op jit(solution)/shard_map/dot_general | solution.py:26
  154.0 4.7 %convolution_bitcast_fusion = f32[1440,1440]{1,0:T(8,128)} fusion(bf16[128,1440]{0,1:T(8,128)(2,1)S(1)} %get-tuple-element.8, bf16[128,1440]{1,0:T(8,128)(2,1)S(1)} %scatter_custom_fusion.2), kind=kOutput, calls=%fused_computation.9 | convolution fusion | flops 530841600 | bytes 9031680
  158.8 5.1 %convolution_bitcast_fusion.1 = f32[1440,1440]{1,0:T(8,128)} fusion(bf16[128,1440]{0,1:T(8,128)(2,1)S(1)} %get-tuple-element.9, bf16[128,1440]{1,0:T(8,128)(2,1)S(1)} %scatter_custom_fusion.2), kind=kOutput, calls=%fused_computation.10 | convolution fusion | flops 530841600 | bytes 9031680
  164.2 6.6 %fusion.37 = f32[1440,1440]{1,0:T(8,128)} fusion(bf16[128,1440]{0,1:T(8,128)(2,1)S(1)} %get-tuple-element.10, bf16[128,1440]{1,0:T(8,128)(2,1)S(1)} %scatter_custom_fusion.4), kind=kOutput, calls=%fused_computation.66 | convolution fusion | flops 530841600 | bytes 9031680 | tf_op jit(solution)/shard_map/dot_general | solution.py:26
  170.8 3.9 %fusion.4 = f32[128,1440]{0,1:T(8,128)S(1)} fusion(bf16[128,1440]{0,1:T(8,128)(2,1)S(1)} %get-tuple-element.9, bf16[1,1440,1440]{2,1,0:T(8,128)(2,1)} %copy.46), kind=kOutput, calls=%fused_computation.15 | convolution fusion | flops 530841600 | bytes 5253120 | tf_op jit(solution)/shard_map/dot_general | solution.py:26
  174.7 3.6 %fusion.21 = bf16[128,1440]{0,1:T(8,128)(2,1)S(1)} fusion(f32[128,1440]{0,1:T(8,128)S(1)} %fusion.4, bf16[128,1440]{0,1:T(8,128)(2,1)S(1)} %get-tuple-element.8, bf16[1,1440,1440]{2,1,0:T(8,128)(2,1)} %copy.44), kind=kOutput, calls=%fused_computation.26 | convolution fusion | flops 531210240 | bytes 5621760 | tf_op jit(solution)/shard_map/dot_general | solution.py:26
  178.5 4.2 %fusion.18 = bf16[128,1440]{0,1:T(8,128)(2,1)S(1)} fusion(bf16[128,1440]{0,1:T(8,128)(2,1)S(1)} %get-tuple-element.10, bf16[1,1440,1440]{2,1,0:T(8,128)(2,1)} %all-gather.11.cloned.1.call-done), kind=kOutput, calls=%fused_computation.25 | convolution fusion | flops 531025920 | bytes 4884480 | tf_op jit(solution)/shard_map/dot_general | solution.py:26
  186.4 23.9 %all_to_all.29 = bf16[16,16,1440]{2,1,0:T(8,128)(2,1)S(1)} all-to-all(bf16[16,16,1440]{2,1,0:T(8,128)(2,1)S(1)} %get-tuple-element.12), channel_id=1, replica_groups=mesh['local'=4,'strided'=4,'rep'=2] {'local','strided'}, dimensions={0} | all-to-all | bytes 1474560 | tf_op jit(solution)/shard_map/all_to_all | solution.py:54
  210.3 3.7 %all-to-all-start.4 = ((bf16[16,16,1440]{2,1,0:T(8,128)(2,1)}), bf16[16,16,1440]{2,1,0:T(8,128)(2,1)S(1)}, u32[]{:S(2)}, u32[]{:S(2)}) async-start(bf16[16,16,1440]{2,1,0:T(8,128)(2,1)} %get-tuple-element.11), calls=%async_computation.4 | async-start | bytes 1572864 | tf_op jit(solution)/shard_map/all_to_all | solution.py:70
  217.4 17.5 %all-to-all-done.4 = bf16[16,16,1440]{2,1,0:T(8,128)(2,1)S(1)} async-done(((bf16[16,16,1440]{2,1,0:T(8,128)(2,1)}), bf16[16,16,1440]{2,1,0:T(8,128)(2,1)S(1)}, u32[]{:S(2)}, u32[]{:S(2)}) %all-to-all-start.4) | async-done | bytes 737312 | tf_op jit(solution)/shard_map/all_to_all | solution.py:70
  237.1 4.7 %copy.54 = bf16[1440,720]{1,0:T(8,128)(2,1)} copy(f32[1440,720]{0,1:T(8,128)} %bitcast.82) | data formatting | bytes 6220800
  241.8 4.7 %copy.52 = bf16[1440,720]{1,0:T(8,128)(2,1)} copy(f32[1440,720]{0,1:T(8,128)} %bitcast.83) | data formatting | bytes 6220800
  246.5 3.9 %convert_bitcast_fusion = bf16[1,720,1440]{2,1,0:T(8,128)(2,1)} fusion(f32[720,1440]{1,0:T(8,128)} %reduce-scatter.8.cloned.1.call-done), kind=kLoop, calls=%fused_computation.27 | loop fusion | flops 1036800 | bytes 6220800 | tf_op jit(solution)/shard_map/broadcast_in_dim | solution.py:163
  (77 shorter events, 26.8 us)
Async XLA Ops:
  7.2 12.4 %copy-start.1 = (bf16[1,1440,720]{2,1,0:T(8,128)(2,1)S(1)}, bf16[1,1440,720]{2,1,0:T(8,128)(2,1)}, u32[]{:S(2)}) copy-start(bf16[1,1440,720]{2,1,0:T(8,128)(2,1)} %param.13) | copy-start | bytes 6220804
  7.2 91.6 %all-gather.7.cloned.1.call-start = ((), (), s32[]{:S(2)}) async-start(), calls=%async_computation.9 | async-start | bytes 13271040 | tf_op jit(solution)/shard_map/all_gather | solution.py:124
  19.5 101.5 %all-gather.9.cloned.1.call-start = ((), (), s32[]{:S(2)}) async-start(), calls=%async_computation.10 | async-start | bytes 13271040 | tf_op jit(solution)/shard_map/all_gather | solution.py:123
  28.8 0.8 copy-start.5
  28.8 1.2 copy-start.6
  28.8 11.9 %copy-start.3 = (bf16[1,32,1440]{2,1,0:T(8,128)(2,1)S(1)}, bf16[1,32,1440]{2,1,0:T(8,128)(2,1)}, u32[]{:S(2)}) copy-start(bf16[1,32,1440]{2,1,0:T(8,128)(2,1)} %param.8) | copy-start | bytes 276484
  28.8 22.7 %copy-start.2 = (bf16[1,32,1440]{2,1,0:T(8,128)(2,1)S(1)}, bf16[1,32,1440]{2,1,0:T(8,128)(2,1)}, u32[]{:S(2)}) copy-start(bf16[1,32,1440]{2,1,0:T(8,128)(2,1)} %param.12) | copy-start | bytes 276484
  28.9 23.1 %copy-start.4 = (f32[1,32,4]{1,2,0:T(4,128)S(1)}, f32[1,32,4]{1,2,0:T(4,128)}, u32[]{:S(2)}) copy-start(f32[1,32,4]{1,2,0:T(4,128)} %param.11) | copy-start | bytes 1540
  28.9 121.3 %all-gather.11.cloned.1.call-start = ((), (), s32[]{:S(2)}) async-start(), calls=%async_computation.11 | async-start | bytes 6635520 | tf_op jit(solution)/shard_map/all_gather | solution.py:125
  32.4 15.5 %all-to-all-start = ((s32[16,1,16]{2,1,0:T(1,128)}), s32[16,1,16]{2,1,0:T(1,128)S(1)}, u32[]{:S(2)}, u32[]{:S(2)}) async-start(s32[16,1,16]{2,1,0:T(1,128)} %all_to_all.18), calls=%async_computation | async-start | bytes 16384 | tf_op jit(solution)/shard_map/all_to_all | solution.py:42
  47.9 24.3 %all-to-all-start.1 = ((bf16[16,16,1440]{2,1,0:T(8,128)(2,1)}), bf16[16,16,1440]{2,1,0:T(8,128)(2,1)S(1)}, u32[]{:S(2)}, u32[]{:S(2)}) async-start(bf16[16,16,1440]{2,1,0:T(8,128)(2,1)} %bitcast.7), calls=%async_computation.1 | async-start | bytes 1572864 | tf_op jit(solution)/shard_map/all_to_all | solution.py:42
  72.1 24.6 %all-to-all-start.3 = ((bf16[16,16,1440]{2,1,0:T(8,128)(2,1)}), bf16[16,16,1440]{2,1,0:T(8,128)(2,1)S(1)}, u32[]{:S(2)}, u32[]{:S(2)}) async-start(bf16[16,16,1440]{2,1,0:T(8,128)(2,1)} %bitcast.17), calls=%async_computation.3 | async-start | bytes 1572864 | tf_op jit(solution)/shard_map/all_to_all | solution.py:62
  75.7 161.3 %reduce-scatter.12.cloned.1.call-start = ((), (), s32[]{:S(2)}) async-start(), calls=%async_computation.13 | async-start | bytes 13271040
  143.3 4.0 %copy-start = (bf16[1,1440,1440]{2,1,0:T(8,128)(2,1)S(1)}, bf16[1,1440,1440]{2,1,0:T(8,128)(2,1)}, u32[]{:S(2)}) copy-start(bf16[1,1440,1440]{2,1,0:T(8,128)(2,1)} %copy.46) | copy-start | bytes 12441604
  158.8 83.0 %reduce-scatter.10.cloned.1.call-start = ((), (), s32[]{:S(2)}) async-start(), calls=%async_computation.12 | async-start | bytes 13271040
  163.9 82.6 %reduce-scatter.8.cloned.1.call-start = ((), (), s32[]{:S(2)}) async-start(), calls=%async_computation.8 | async-start | bytes 13271040 | tf_op jit(solution)/shard_map/reduce_scatter | solution.py:149
  210.3 24.6 %all-to-all-start.4 = ((bf16[16,16,1440]{2,1,0:T(8,128)(2,1)}), bf16[16,16,1440]{2,1,0:T(8,128)(2,1)S(1)}, u32[]{:S(2)}, u32[]{:S(2)}) async-start(bf16[16,16,1440]{2,1,0:T(8,128)(2,1)} %get-tuple-element.11), calls=%async_computation.4 | async-start | bytes 1572864 | tf_op jit(solution)/shard_map/all_to_all | solution.py:70
Sparse Core Ops, SparseCore 0:
  19.6 23.8 all-gather.6
  45.1 22.3 all-gather.8
  69.0 15.1 all-gather.10
  158.9 14.3 reduce-scatter.11
  175.6 18.4 reduce-scatter.9
  196.3 18.4 reduce-scatter.7
where the time goes:
time: 259 us; the launch traced here: 257 us
  local copies, waits for them, and re-layouts  91.1 us (35%)
  waiting for transfers between devices  58.5 us (23%)
  matrix products  38.6 us (15%)
  blocking collectives  23.9 us (9%)
  starting transfers between devices  19.7 us (8%)
  between operations  14.4 us (6%)
  other arithmetic  11 us (4%)
    unnamed x21, local copies, waits for them, and re-layouts  31.3 us
    dot_general x7, matrix products, contract(): lax.dot_general(left, right, (((left_dim,), (right_dim,)), ((), ())), pre...  28.9 us
    all_to_all x1, blocking collectives, return_outputs(): lax.all_to_all(split_flat(rows), ('local', 'strided'), split_axis=0, conc...  23.9 us
    all_to_all x2, waiting for transfers between devices, dispatch_rows(): lax.all_to_all(for_sending(tuple((split_flat(item) for item in payload)))...  22.5 us
    all_gather x1, local copies, waits for them, and re-layouts, local(): lax.all_gather(gate_shard, 'rep', axis=1, tiled=True)  22.3 us
    all_gather x1, local copies, waits for them, and re-layouts, local(): lax.all_gather(up_shard, 'rep', axis=1, tiled=True)  22.2 us
    all_to_all x1, waiting for transfers between devices, dispatch_grads(): lax.all_to_all(split_flat(rows), ('local', 'strided'), split_axis=0, conc...  17.8 us
    all_to_all x1, waiting for transfers between devices, return_grads(): lax.all_to_all(split_flat(rows), ('local', 'strided'), split_axis=0, conc...  17.5 us
  transfers between devices with their start and end apart: 10, of which 4 were waited for; matrix products, arithmetic and copies ran while one was open for 45% of the time, Pallas kernels for 0%

commit v1 on v0

v1 whole, which is shorter than its diff:
```python
import functools

import jax
import jax.numpy as jnp
from jax import lax
from jax.experimental import pallas as pl
from jax.experimental.pallas import tpu as pltpu
from jax.sharding import PartitionSpec as P

SWIGLU_ALPHA = 1.702
BF = jnp.bfloat16
F32 = jnp.float32
MESH = pl.DeviceIdType.MESH


def contract(left, right, left_dim, right_dim):
    return lax.dot_general(
        left, right, (((left_dim,), (right_dim,)), ((), ())), preferred_element_type=F32
    )


def xor(index, constant, size):
    result, bit = 0, 1
    while bit < size:
        result = result + bit * lax.rem(lax.div(index, bit) + (constant // bit) % 2, 2)
        bit *= 2
    return result


def three_parts(value):
    high = value.astype(BF).astype(F32)
    middle = (value - high).astype(BF).astype(F32)
    low = (value - high - middle).astype(BF).astype(F32)
    return high, middle, low


def kernel(
    sizes,
    tokens,
    experts,
    slots,
    router,
    out_grad,
    gate_hbm,
    up_hbm,
    down_hbm,
    mixed,
    token_grad,
    weight_grad,
    gate_grad_hbm,
    up_grad_hbm,
    down_grad_hbm,
    w_gate,
    w_up,
    w_down,
    d_gate,
    d_up,
    d_down,
    gathered,
    plane_out,
    plane_in,
    back_out,
    back_in,
    home_out,
    home_in,
    select,
    place,
    rows,
    grads,
    hidden,
    gate_pre,
    up_pre,
    slope_gate,
    slope_up,
    partial,
    other,
    reply,
    w_sem,
    d_sem,
    z_send,
    z_recv,
    p_send,
    p_recv,
    r_send,
    r_recv,
    h_send,
    h_recv,
    c_send,
    c_recv,
):
    S, L, T, TOP, PM, G, R, D, DP, CAP = sizes
    NG, TT, LR = S // G, G * T, L * R
    TB = DP - 128
    OFF = D - TB
    l, s, r = lax.axis_index("local"), lax.axis_index("strided"), lax.axis_index("rep")
    twin = 1 - r
    strided_peers = [xor(s, j, S) for j in range(S)]
    local_peers = [xor(l, j, L) for j in range(L)]
    groups = [xor(lax.div(s, G), j, NG) for j in range(NG)]

    loads = [
        pltpu.make_async_copy(source.at[0], target, w_sem.at[i])
        for i, (source, target) in enumerate(
            ((gate_hbm, w_gate), (up_hbm, w_up), (down_hbm, w_down))
        )
    ]
    for load in loads:
        load.start()

    barrier = pltpu.get_barrier_semaphore()
    for j in range(1, S):
        pl.semaphore_signal(
            barrier, inc=1, device_id=(l, strided_peers[j], r), device_id_type=MESH
        )
    for j in range(1, L):
        pl.semaphore_signal(barrier, inc=1, device_id=(local_peers[j], s, r), device_id_type=MESH)
    pl.semaphore_signal(barrier, inc=1, device_id=(l, s, twin), device_id_type=MESH)

    lane = lax.broadcasted_iota(jnp.int32, (T, 128), 1) - OFF
    gathered[0, s, :, TB:] = jnp.zeros((T, 128), BF)
    gathered[1, s, :, TB:] = jnp.zeros((T, 128), BF)
    gathered[0, s, :, :D] = tokens[0]
    gathered[1, s, :, :D] = out_grad[0]
    tail = gathered[0, s, :, TB:].astype(F32)
    named = experts[0].astype(F32)
    slotted = slots[0].astype(F32) + 1.0
    parts = (named, slotted) + three_parts(router[0])
    for i, part in enumerate(parts):
        for k in range(TOP):
            tail = jnp.where(lane == i * TOP + k, part[:, k : k + 1], tail)
    gathered[0, s, :, TB:] = tail.astype(BF)

    pl.semaphore_wait(barrier, (S - 1) + (L - 1) + 1)

    pending = []

    def send(source, target, send_sem, recv_sem, device):
        copy = pltpu.make_async_remote_copy(
            src_ref=source,
            dst_ref=target,
            send_sem=send_sem,
            recv_sem=recv_sem,
            device_id=device,
            device_id_type=MESH,
        )
        copy.start()
        pending.append(copy)
        return copy

    def arrival(target, send_sem, recv_sem, device):
        return pltpu.make_async_remote_copy(
            src_ref=target,
            dst_ref=target,
            send_sem=send_sem,
            recv_sem=recv_sem,
            device_id=device,
            device_id_type=MESH,
        )

    for kind in range(2):
        for j in range(1, S):
            send(
                gathered.at[kind, s],
                gathered.at[kind, s],
                z_send.at[kind, j],
                z_recv.at[kind, s],
                (l, strided_peers[j], r),
            )

    def await_strided(kind, buffer, sends, recvs, j):
        peer = strided_peers[j]
        arrival(
            buffer.at[kind, peer], sends.at[kind, j], recvs.at[kind, peer], (l, peer, r)
        ).wait_recv()

    def await_local(kind, buffer, sends, recvs, group, j):
        peer = local_peers[j]
        arrival(
            buffer.at[kind, group, peer],
            sends.at[kind, group, j],
            recvs.at[kind, group, peer],
            (peer, s, r),
        ).wait_recv()

    def send_local(kind, outgoing, incoming, sends, recvs, group):
        for j in range(1, L):
            send(
                outgoing.at[kind, group, local_peers[j]],
                incoming.at[kind, group, l],
                sends.at[kind, group, j],
                recvs.at[kind, group, l],
                (local_peers[j], s, r),
            )
        incoming[kind, group, l] = outgoing[kind, group, l]

    column = lax.broadcasted_iota(jnp.int32, (TT, LR), 1)
    token = lax.broadcasted_iota(jnp.int32, (TT, LR), 0)
    wanted = (lax.div(column, R) * S + s).astype(F32)
    same_source = lax.div(token, T) == lax.div(lax.rem(column, R), PM)
    rank_wanted = lax.rem(column, PM).astype(F32)
    below = (
        lax.broadcasted_iota(jnp.int32, (TT, TT), 1) < lax.broadcasted_iota(jnp.int32, (TT, TT), 0)
    ).astype(F32).astype(BF)
    group_lane = lax.broadcasted_iota(jnp.int32, (TT, 128), 1) - OFF
    row_lane = lax.broadcasted_iota(jnp.int32, (LR, 128), 1) - OFF

    for jg in range(NG):
        group = groups[jg]
        for j in range(max(1, jg * G), (jg + 1) * G):
            await_strided(0, gathered, z_send, z_recv, j)
        block = gathered[0, pl.ds(group * G, G)].reshape(TT, DP)
        route = block[:, TB:].astype(F32)

        def lane_of(i, k):
            return route[:, OFF + i * TOP + k : OFF + i * TOP + k + 1]

        hits = []
        for k in range(TOP):
            hit = (lane_of(0, k) == wanted) & (lane_of(1, k) > 0.0) & same_source
            hits.append(hit.astype(F32))
        hit_any = sum(hits)
        rank = contract(below, hit_any.astype(BF), 1, 0)
        picked = jnp.where(rank == rank_wanted, hit_any, 0.0)
        picked_bf = picked.astype(BF)
        select[group] = picked_bf
        moved = contract(picked_bf, block, 0, 0)
        info = jnp.zeros((LR, 128), F32)
        for k in range(TOP):
            values = jnp.where(group_lane == 0, lane_of(1, k), 0.0)
            values = jnp.where(group_lane == 1, float(k), values)
            for i in range(3):
                values = jnp.where(group_lane == 2 + i, lane_of(2 + i, k), values)
            info = info + contract((picked * hits[k]).astype(BF), values.astype(BF), 0, 0)
        plane_out[0, group, :, :, :TB] = moved[:, :TB].astype(BF).reshape(L, R, TB)
        plane_out[0, group, :, :, TB:] = (
            jnp.where(row_lane < 0, moved[:, TB:], info).astype(BF).reshape(L, R, 128)
        )
        send_local(0, plane_out, plane_in, p_send, p_recv, group)

    for jg in range(NG):
        group = groups[jg]
        for j in range(max(1, jg * G), (jg + 1) * G):
            await_strided(1, gathered, z_send, z_recv, j)
        block = gathered[1, pl.ds(group * G, G)].reshape(TT, DP)
        moved = contract(select[group], block, 0, 0)
        plane_out[1, group] = moved.astype(BF).reshape(L, R, DP)
        send_local(1, plane_out, plane_in, p_send, p_recv, group)

    def swap(index, source, target):
        copy = send(source, target, c_send.at[index], c_recv.at[index], (l, s, twin))
        return copy

    def await_plane(kind):
        for jg in range(NG):
            for j in range(1, L):
                await_local(kind, plane_in, p_send, p_recv, groups[jg], j)

    await_plane(0)
    received = plane_in[0].reshape(NG * LR, DP)
    slot_of = received[:, TB:].astype(F32)[:, OFF : OFF + 1]
    slot_lane = lax.broadcasted_iota(jnp.int32, (NG * LR, CAP), 1).astype(F32) + 1.0
    place[...] = (slot_of == slot_lane).astype(F32).astype(BF)
    rows[0, r] = contract(place[...], received, 0, 0).astype(BF)
    swap(0, rows.at[0, r], rows.at[0, r])
    for load in loads:
        load.wait()
    arrival(rows.at[0, twin], c_send.at[0], c_recv.at[0], (l, s, twin)).wait_recv()

    x = rows[0].reshape(2 * CAP, DP)[:, :D]
    gate = contract(x, w_gate[...], 1, 0)
    gate_pre[...] = gate
    up = contract(x, w_up[...], 1, 0)
    up_pre[...] = up
    hidden[...] = ((up + 1.0) * gate * jax.nn.sigmoid(SWIGLU_ALPHA * gate)).astype(BF)
    partial[0] = contract(hidden[...], w_down[...], 1, 0).reshape(2, CAP, D)
    swap(1, partial.at[0, twin], other.at[0])

    def weight_of(tail):
        return (
            tail[:, OFF + 2 : OFF + 3] + tail[:, OFF + 3 : OFF + 4] + tail[:, OFF + 4 : OFF + 5]
        )

    weight_rows = weight_of(rows[0].reshape(2 * CAP, DP)[:, TB:].astype(F32))
    own_tail = rows[0, r, :, TB:].astype(F32)
    arrival(other.at[0], c_send.at[1], c_recv.at[1], (l, s, twin)).wait_recv()
    out = partial[0, r] + other[0]
    reply[0, :, TB:] = jnp.zeros((CAP, 128), BF)
    reply[0, :, :D] = (weight_of(own_tail) * out).astype(BF)
    back_out[0] = contract(place[...], reply[0], 1, 0).astype(BF).reshape(NG, L, R, DP)
    for jg in reversed(range(NG)):
        send_local(0, back_out, back_in, r_send, r_recv, groups[jg])

    await_plane(1)
    rows[1, r] = contract(place[...], plane_in[1].reshape(NG * LR, DP), 0, 0).astype(BF)
    swap(2, rows.at[1, r], rows.at[1, r])
    own_grads = rows[1, r, :, :D].astype(F32)
    router_grad = jnp.sum(own_grads * out, axis=1, keepdims=True)
    slot_tail = lax.broadcasted_iota(jnp.int32, (CAP, 128), 1).astype(F32) - float(OFF)
    which = own_tail[:, OFF + 1 : OFF + 2]
    reply_tail = jnp.zeros((CAP, 128), F32)
    for i, part in enumerate(three_parts(router_grad)):
        reply_tail = jnp.where(slot_tail == which + float(i * TOP), part, reply_tail)
    arrival(rows.at[1, twin], c_send.at[2], c_recv.at[2], (l, s, twin)).wait_recv()
    grads[...] = (weight_rows * rows[1].reshape(2 * CAP, DP)[:, :D].astype(F32)).astype(BF)
    grad_hidden = contract(grads[...], w_down[...], 1, 1)
    gate = gate_pre[...]
    sig = jax.nn.sigmoid(SWIGLU_ALPHA * gate)
    slope_up[...] = (grad_hidden * gate * sig).astype(BF)
    slope = sig + SWIGLU_ALPHA * gate * sig * (1.0 - sig)
    slope_gate[...] = (grad_hidden * (up_pre[...] + 1.0) * slope).astype(BF)
    partial[1] = (
        contract(slope_gate[...], w_gate[...], 1, 1) + contract(slope_up[...], w_up[...], 1, 1)
    ).reshape(2, CAP, D)
    swap(3, partial.at[1, twin], other.at[1])

    stores = []

    def store(index, source, target):
        copy = pltpu.make_async_copy(source, target.at[0], d_sem.at[index])
        copy.start()
        stores.append(copy)

    d_down[...] = contract(hidden[...], grads[...], 0, 0).astype(BF)
    store(2, d_down, down_grad_hbm)

    arrival(other.at[1], c_send.at[3], c_recv.at[3], (l, s, twin)).wait_recv()
    reply[1, :, TB:] = jnp.zeros((CAP, 128), BF)
    reply[1, :, :D] = (partial[1, r] + other[1]).astype(BF)
    reply[1, :, TB:] = jnp.where(
        slot_tail < 0.0, reply[1, :, TB:].astype(F32), reply_tail
    ).astype(BF)
    back_out[1] = contract(place[...], reply[1], 1, 0).astype(BF).reshape(NG, L, R, DP)
    for jg in reversed(range(NG)):
        send_local(1, back_out, back_in, r_send, r_recv, groups[jg])

    def send_home(kind):
        for jg in reversed(range(NG)):
            group = groups[jg]
            for j in range(1, L):
                await_local(kind, back_in, r_send, r_recv, group, j)
            total = contract(select[group], back_in[kind, group].reshape(LR, DP), 1, 0)
            home_out[kind, pl.ds(group * G, G)] = total.astype(BF).reshape(G, T, DP)
            for j in range(jg * G, (jg + 1) * G):
                peer = strided_peers[j]
                if j == 0:
                    home_in[kind, s] = home_out[kind, s]
                else:
                    send(
                        home_out.at[kind, peer],
                        home_in.at[kind, s],
                        h_send.at[kind, j],
                        h_recv.at[kind, s],
                        (l, peer, r),
                    )

    send_home(0)
    x = rows[0].reshape(2 * CAP, DP)[:, :D]
    d_gate[...] = contract(x, slope_gate[...], 0, 0).astype(BF)
    store(0, d_gate, gate_grad_hbm)
    d_up[...] = contract(x, slope_up[...], 0, 0).astype(BF)
    store(1, d_up, up_grad_hbm)
    send_home(1)

    def collect(kind):
        for j in range(1, S):
            await_strided(kind, home_in, h_send, h_recv, j)
        total = home_in[kind, 0].astype(F32)
        for j in range(1, S):
            total = total + home_in[kind, j].astype(F32)
        return total

    mixed[0] = collect(0)[:, :D].astype(BF)
    total = collect(1)
    token_grad[0] = total[:, :D].astype(BF)
    tail = total[:, TB:]
    weight_grad[0] = tail[:, OFF : OFF + TOP] + (
        tail[:, OFF + TOP : OFF + 2 * TOP] + tail[:, OFF + 2 * TOP : OFF + 3 * TOP]
    )
    for copy in stores:
        copy.wait()
    for copy in pending:
        copy.wait_send()


def local(tokens, experts, slots, route_weight, out_grad, w_gate, w_up, w_down):
    L, S = lax.axis_size("local"), lax.axis_size("strided")
    T, D = tokens.shape[1:]
    TOP = experts.shape[2]
    F = w_gate.shape[2]
    CAP = T * TOP
    PM = 2 * CAP // (L * S)
    G = max(1, 16 // PM)
    R = G * PM
    NG, TT, LR = S // G, G * T, L * R
    DP = -(-(D + 5 * TOP) // 128) * 128
    sizes = (S, L, T, TOP, PM, G, R, D, DP, CAP)
    vmem = pl.BlockSpec(memory_space=pltpu.VMEM)
    anywhere = pl.BlockSpec(memory_space=pl.ANY)
    dma = pltpu.SemaphoreType.DMA
    return pl.pallas_call(
        functools.partial(kernel, sizes),
        out_shape=(
            jax.ShapeDtypeStruct((1, T, D), BF),
            jax.ShapeDtypeStruct((1, T, D), BF),
            jax.ShapeDtypeStruct((1, T, TOP), F32),
            jax.ShapeDtypeStruct((1, D, F), BF),
            jax.ShapeDtypeStruct((1, D, F), BF),
            jax.ShapeDtypeStruct((1, F, D), BF),
        ),
        in_specs=[vmem] * 5 + [anywhere] * 3,
        out_specs=[vmem] * 3 + [anywhere] * 3,
        scratch_shapes=[
            pltpu.VMEM((D, F), BF),
            pltpu.VMEM((D, F), BF),
            pltpu.VMEM((F, D), BF),
            pltpu.VMEM((D, F), BF),
            pltpu.VMEM((D, F), BF),
            pltpu.VMEM((F, D), BF),
            pltpu.VMEM((2, S, T, DP), BF),
            pltpu.VMEM((2, NG, L, R, DP), BF),
            pltpu.VMEM((2, NG, L, R, DP), BF),
            pltpu.VMEM((2, NG, L, R, DP), BF),
            pltpu.VMEM((2, NG, L, R, DP), BF),
            pltpu.VMEM((2, S, T, DP), BF),
            pltpu.VMEM((2, S, T, DP), BF),
            pltpu.VMEM((NG, TT, LR), BF),
            pltpu.VMEM((NG * LR, CAP), BF),
            pltpu.VMEM((2, 2, CAP, DP), BF),
            pltpu.VMEM((2 * CAP, D), BF),
            pltpu.VMEM((2 * CAP, F), BF),
            pltpu.VMEM((2 * CAP, F), F32),
            pltpu.VMEM((2 * CAP, F), F32),
            pltpu.VMEM((2 * CAP, F), BF),
            pltpu.VMEM((2 * CAP, F), BF),
            pltpu.VMEM((2, 2, CAP, D), F32),
            pltpu.VMEM((2, CAP, D), F32),
            pltpu.VMEM((2, CAP, DP), BF),
            dma((3,)),
            dma((3,)),
            dma((2, S)),
            dma((2, S)),
            dma((2, NG, L)),
            dma((2, NG, L)),
            dma((2, NG, L)),
            dma((2, NG, L)),
            dma((2, S)),
            dma((2, S)),
            dma((4,)),
            dma((4,)),
        ],
        compiler_params=pltpu.CompilerParams(
            collective_id=0, has_side_effects=True, vmem_limit_bytes=58 * 1024 * 1024
        ),
        cost_estimate=pl.CostEstimate(
            flops=18 * 2 * CAP * D * F, bytes_accessed=12 * D * F, transcendentals=4 * CAP * F
        ),
        name="moe_layer",
    )(tokens, experts, slots, route_weight, out_grad, w_gate, w_up, w_down)


def solution(mesh):
    pairs = P("rep", ("local", "strided"), None)
    split_last = P(("local", "strided"), None, "rep")
    split_middle = P(("local", "strided"), "rep", None)
    return jax.shard_map(
        local,
        mesh=mesh,
        in_specs=(pairs,) * 5 + (split_last, split_last, split_middle),
        out_specs=(pairs,) * 3 + (split_last, split_last, split_middle),
        check_vma=False,
    )
```

time: 259 us -> 75.7 us (0.29)
  local copies, waits for them, and re-layouts: 91.1 us -> 15.6 us
  Pallas kernels: 0 us -> 59.1 us
  waiting for transfers between devices: 58.5 us -> 0 us
  matrix products: 38.6 us -> 0 us
  blocking collectives: 23.9 us -> 0 us
  starting transfers between devices: 19.7 us -> 0 us
  between operations: 14.4 us -> 0.65 us
  other arithmetic: 11 us -> 0 us
    pallas_call x0 -> x1, Pallas kernels: none -> 59.1 us  [local(): pl.pallas_call(functools.partial(kernel, sizes), out_shape=(jax.ShapeDtyp...]
    all_to_all x4 -> x0, waiting for transfers between devices: 57.7 us -> none  [the longest x2 22.5 us: dispatch_rows(): lax.all_to_all(for_sending(tuple((split_flat(item) for item in payload)))...]
    all_gather x2 -> x0, local copies, waits for them, and re-layouts: 44.5 us -> none  [the longest x1 22.3 us: local(): lax.all_gather(gate_shard, 'rep', axis=1, tiled=True)]
    dot_general x7 -> x0, matrix products: 28.9 us -> none  [contract(): lax.dot_general(left, right, (((left_dim,), (right_dim,)), ((), ())), pre...]
    all_to_all x1 -> x0, blocking collectives: 23.9 us -> none  [return_outputs(): lax.all_to_all(split_flat(rows), ('local', 'strided'), split_axis=0, conc...]
    all_to_all x4 -> x0, starting transfers between devices: 19.2 us -> none  [the longest x2 11.9 us: dispatch_rows(): lax.all_to_all(for_sending(tuple((split_flat(item) for item in payload)))...]
    unnamed x21 -> x12, local copies, waits for them, and re-layouts: 31.3 us -> 14.2 us
    unnamed x2 -> x0, matrix products: 9.78 us -> none
  transfers between devices with their start and end apart: 10 -> 0, of which waited for: 4 -> 0; matrix products, arithmetic and copies ran while one was open for 45% -> 0% of each run, Pallas kernels for 0% -> 0%
where the time goes in v1:
time: 75.7 us; the launch traced here: 75.3 us
  Pallas kernels  59.1 us (78%)
  local copies, waits for them, and re-layouts  15.6 us (21%)
    pallas_call x1, Pallas kernels, local(): pl.pallas_call(functools.partial(kernel, sizes), out_shape=(jax.ShapeDtyp...  59.1 us
    unnamed x12, local copies, waits for them, and re-layouts  14.2 us

profile of v1, /device:TPU:0, one launch (start us, length us, event | category | flops | bytes accessed | tf_op | source)
XLA Modules:
  0.0 75.3 jit_solution(7525206052066865901)
XLA Ops:
  0.6 1.4 %copy.14.experts = s32[1,32,4]{2,1,0:T(8,128)} copy(s32[1,32,4]{1,2,0:T(4,128)} %param.9) | data formatting | bytes 1024 | tf_op args[1]
  2.0 1.4 %copy.15.slots = s32[1,32,4]{2,1,0:T(8,128)} copy(s32[1,32,4]{1,2,0:T(4,128)} %param.10) | data formatting | bytes 1024 | tf_op args[2]
  3.4 1.4 %copy.16.router = f32[1,32,4]{2,1,0:T(8,128)} copy(f32[1,32,4]{1,2,0:T(4,128)} %param.11) | data formatting | bytes 1024 | tf_op args[3]
  4.7 59.1 %moe_layer.1 = (bf16[1,32,1440]{2,1,0:T(8,128)(2,1)}, bf16[1,32,1440]{2,1,0:T(8,128)(2,1)}, f32[1,32,4]{2,1,0:T(8,128)}, bf16[1,1440,720]{2,1,0:T(8,128)(2,1)}, ...) custom-call(bf16[1,32,1440]{2,1,0:T(8,128)(2,1)} %tokens.1, s32[1,32,4]{2,1,0:T(8,128)} %copy.14.experts, ...), custom_call_target="tpu_custom_call" | custom-call | flops 4777574400 | bytes 12441600 | tf_op jit(solution)/shard_map/moe_layer/pallas_call | solution.py:400
  63.8 1.4 %copy.17 = f32[1,32,4]{1,2,0:T(4,128)} copy(f32[1,32,4]{2,1,0:T(8,128)} %get-tuple-element.8) | data formatting | bytes 1024 | tf_op jit(solution)/shard_map/moe_layer/pallas_call | solution.py:400
  65.2 1.5 %copy.23 = bf16[1,32,1440]{2,1,0:T(8,128)(2,1)} copy(bf16[1,32,1440]{2,1,0:T(8,128)(2,1)} %get-tuple-element.18) | data formatting | bytes 184320
  66.7 1.5 %copy.24 = bf16[1,32,1440]{2,1,0:T(8,128)(2,1)} copy(bf16[1,32,1440]{2,1,0:T(8,128)(2,1)} %get-tuple-element.19) | data formatting | bytes 184320
  68.3 0.0 copy-start.1
  68.3 3.3 %copy.25 = bf16[1,1440,720]{2,1,0:T(8,128)(2,1)} copy(bf16[1,1440,720]{2,1,0:T(8,128)(2,1)} %get-tuple-element.21) | data formatting | bytes 4147200
  71.5 0.0 copy-done.1
  71.5 0.0 copy-start
  71.5 1.4 %copy.26 = bf16[1,1440,720]{2,1,0:T(8,128)(2,1)} copy(bf16[1,1440,720]{2,1,0:T(8,128)(2,1)S(1)} %copy-done.1) | data formatting | bytes 4147200
  72.9 1.1 %copy-done = bf16[1,720,1440]{2,1,0:T(8,128)(2,1)S(1)} copy-done((bf16[1,720,1440]{2,1,0:T(8,128)(2,1)S(1)}, bf16[1,720,1440]{2,1,0:T(8,128)(2,1)}, u32[]{:S(2)}) %copy-start) | copy-done | bytes 2073624
  74.0 1.4 %copy.27 = bf16[1,720,1440]{2,1,0:T(8,128)(2,1)} copy(bf16[1,720,1440]{2,1,0:T(8,128)(2,1)S(1)} %copy-done) | data formatting | bytes 4147200
Async XLA Ops:
  68.3 3.3 %copy-start.1 = (bf16[1,1440,720]{2,1,0:T(8,128)(2,1)S(1)}, bf16[1,1440,720]{2,1,0:T(8,128)(2,1)}, u32[]{:S(2)}) copy-start(bf16[1,1440,720]{2,1,0:T(8,128)(2,1)} %get-tuple-element.22) | copy-start | bytes 6220804
  71.5 2.4 %copy-start = (bf16[1,720,1440]{2,1,0:T(8,128)(2,1)S(1)}, bf16[1,720,1440]{2,1,0:T(8,128)(2,1)}, u32[]{:S(2)}) copy-start(bf16[1,720,1440]{2,1,0:T(8,128)(2,1)} %get-tuple-element.23) | copy-start | bytes 6220804

commit v2 on v1

--- a/solution.py
+++ b/solution.py
@@ -47,15 +47,15 @@
     mixed,
     token_grad,
     weight_grad,
-    gate_grad_hbm,
-    up_grad_hbm,
-    down_grad_hbm,
+    rows_hbm,
+    grads_hbm,
+    hidden_hbm,
+    slope_gate_hbm,
+    slope_up_hbm,
     w_gate,
     w_up,
     w_down,
-    d_gate,
-    d_up,
-    d_down,
+    routing,
     gathered,
     plane_out,
     plane_in,
@@ -121,14 +121,16 @@
     gathered[1, s, :, TB:] = jnp.zeros((T, 128), BF)
     gathered[0, s, :, :D] = tokens[0]
     gathered[1, s, :, :D] = out_grad[0]
+    routing[...] = jnp.zeros(routing.shape, F32)
+    parts = (experts[0].astype(F32), slots[0].astype(F32) + 1.0) + three_parts(router[0])
+    for i, part in enumerate(parts):
+        routing[i * 16 : i * 16 + TOP, :] = part
+    line = lax.broadcasted_iota(jnp.int32, (80, 128), 0)
+    spot = lax.broadcasted_iota(jnp.int32, (80, 128), 1) - OFF
+    spread = (lax.rem(line, 16) < TOP) & (spot == lax.div(line, 16) * TOP + lax.rem(line, 16))
+    info = contract(routing[...].astype(BF), spread.astype(F32).astype(BF), 0, 0)
     tail = gathered[0, s, :, TB:].astype(F32)
-    named = experts[0].astype(F32)
-    slotted = slots[0].astype(F32) + 1.0
-    parts = (named, slotted) + three_parts(router[0])
-    for i, part in enumerate(parts):
-        for k in range(TOP):
-            tail = jnp.where(lane == i * TOP + k, part[:, k : k + 1], tail)
-    gathered[0, s, :, TB:] = tail.astype(BF)
+    gathered[0, s, :, TB:] = jnp.where(lane < 0, tail, info).astype(BF)
 
     pl.semaphore_wait(barrier, (S - 1) + (L - 1) + 1)
 
@@ -157,15 +159,17 @@
             device_id_type=MESH,
         )
 
-    for kind in range(2):
-        for j in range(1, S):
-            send(
-                gathered.at[kind, s],
-                gathered.at[kind, s],
-                z_send.at[kind, j],
-                z_recv.at[kind, s],
-                (l, strided_peers[j], r),
-            )
+    def send_strided(kind, j):
+        send(
+            gathered.at[kind, s],
+            gathered.at[kind, s],
+            z_send.at[kind, j],
+            z_recv.at[kind, s],
+            (l, strided_peers[j], r),
+        )
+
+    for j in range(1, S):
+        send_strided(0, j)
 
     def await_strided(kind, buffer, sends, recvs, j):
         peer = strided_peers[j]
@@ -208,6 +212,7 @@
         group = groups[jg]
         for j in range(max(1, jg * G), (jg + 1) * G):
             await_strided(0, gathered, z_send, z_recv, j)
+            send_strided(1, j)
         block = gathered[0, pl.ds(group * G, G)].reshape(TT, DP)
         route = block[:, TB:].astype(F32)
 
@@ -250,6 +255,35 @@
         copy = send(source, target, c_send.at[index], c_recv.at[index], (l, s, twin))
         return copy
 
+    middle = -(-D // 256) * 128
+    halves = ((0, middle), (middle, D))
+
+    def swap_half(kind, c):
+        low, high = halves[c]
+        index = 2 + 2 * kind + c
+        swap(
+            index,
+            partial.at[kind, twin, :, pl.ds(low, high - low)],
+            other.at[kind, :, pl.ds(low, high - low)],
+        )
+
+    def await_half(kind, c):
+        low, high = halves[c]
+        index = 2 + 2 * kind + c
+        arrival(
+            other.at[kind, :, pl.ds(low, high - low)],
+            c_send.at[index],
+            c_recv.at[index],
+            (l, s, twin),
+        ).wait_recv()
+
+    saves = []
+
+    def save(index, source, target):
+        copy = pltpu.make_async_copy(source, target, d_sem.at[index])
+        copy.start()
+        saves.append(copy)
+
     def await_plane(kind):
         for jg in range(NG):
             for j in range(1, L):
@@ -272,8 +306,12 @@
     up = contract(x, w_up[...], 1, 0)
     up_pre[...] = up
     hidden[...] = ((up + 1.0) * gate * jax.nn.sigmoid(SWIGLU_ALPHA * gate)).astype(BF)
-    partial[0] = contract(hidden[...], w_down[...], 1, 0).reshape(2, CAP, D)
-    swap(1, partial.at[0, twin], other.at[0])
+    save(2, hidden, hidden_hbm)
+    save(0, rows.at[0], rows_hbm)
+    for c, (low, high) in enumerate(halves):
+        part = contract(hidden[...], w_down[:, low:high], 1, 0)
+        partial[0, :, :, low:high] = part.reshape(2, CAP, high - low)
+        swap_half(0, c)
 
     def weight_of(tail):
         return (
@@ -282,7 +320,8 @@
 
     weight_rows = weight_of(rows[0].reshape(2 * CAP, DP)[:, TB:].astype(F32))
     own_tail = rows[0, r, :, TB:].astype(F32)
-    arrival(other.at[0], c_send.at[1], c_recv.at[1], (l, s, twin)).wait_recv()
+    await_half(0, 0)
+    await_half(0, 1)
     out = partial[0, r] + other[0]
     reply[0, :, TB:] = jnp.zeros((CAP, 128), BF)
     reply[0, :, :D] = (weight_of(own_tail) * out).astype(BF)
@@ -292,7 +331,7 @@
 
     await_plane(1)
     rows[1, r] = contract(place[...], plane_in[1].reshape(NG * LR, DP), 0, 0).astype(BF)
-    swap(2, rows.at[1, r], rows.at[1, r])
+    swap(1, rows.at[1, r], rows.at[1, r])
     own_grads = rows[1, r, :, :D].astype(F32)
     router_grad = jnp.sum(own_grads * out, axis=1, keepdims=True)
     slot_tail = lax.broadcasted_iota(jnp.int32, (CAP, 128), 1).astype(F32) - float(OFF)
@@ -300,7 +339,7 @@
     reply_tail = jnp.zeros((CAP, 128), F32)
     for i, part in enumerate(three_parts(router_grad)):
         reply_tail = jnp.where(slot_tail == which + float(i * TOP), part, reply_tail)
-    arrival(rows.at[1, twin], c_send.at[2], c_recv.at[2], (l, s, twin)).wait_recv()
+    arrival(rows.at[1, twin], c_send.at[1], c_recv.at[1], (l, s, twin)).wait_recv()
     grads[...] = (weight_rows * rows[1].reshape(2 * CAP, DP)[:, :D].astype(F32)).astype(BF)
     grad_hidden = contract(grads[...], w_down[...], 1, 1)
     gate = gate_pre[...]
@@ -308,22 +347,17 @@
     slope_up[...] = (grad_hidden * gate * sig).astype(BF)
     slope = sig + SWIGLU_ALPHA * gate * sig * (1.0 - sig)
     slope_gate[...] = (grad_hidden * (up_pre[...] + 1.0) * slope).astype(BF)
-    partial[1] = (
-        contract(slope_gate[...], w_gate[...], 1, 1) + contract(slope_up[...], w_up[...], 1, 1)
-    ).reshape(2, CAP, D)
-    swap(3, partial.at[1, twin], other.at[1])
-
-    stores = []
-
-    def store(index, source, target):
-        copy = pltpu.make_async_copy(source, target.at[0], d_sem.at[index])
-        copy.start()
-        stores.append(copy)
-
-    d_down[...] = contract(hidden[...], grads[...], 0, 0).astype(BF)
-    store(2, d_down, down_grad_hbm)
-
-    arrival(other.at[1], c_send.at[3], c_recv.at[3], (l, s, twin)).wait_recv()
+    for c, (low, high) in enumerate(halves):
+        part = contract(slope_gate[...], w_gate[low:high, :], 1, 1) + contract(
+            slope_up[...], w_up[low:high, :], 1, 1
+        )
+        partial[1, :, :, low:high] = part.reshape(2, CAP, high - low)
+        swap_half(1, c)
+    save(1, grads, grads_hbm)
+    save(3, slope_gate, slope_gate_hbm)
+    save(4, slope_up, slope_up_hbm)
+    await_half(1, 0)
+    await_half(1, 1)
     reply[1, :, TB:] = jnp.zeros((CAP, 128), BF)
     reply[1, :, :D] = (partial[1, r] + other[1]).astype(BF)
     reply[1, :, TB:] = jnp.where(
@@ -354,11 +388,6 @@
                     )
 
     send_home(0)
-    x = rows[0].reshape(2 * CAP, DP)[:, :D]
-    d_gate[...] = contract(x, slope_gate[...], 0, 0).astype(BF)
-    store(0, d_gate, gate_grad_hbm)
-    d_up[...] = contract(x, slope_up[...], 0, 0).astype(BF)
-    store(1, d_up, up_grad_hbm)
     send_home(1)
 
     def collect(kind):
@@ -372,14 +401,92 @@
     mixed[0] = collect(0)[:, :D].astype(BF)
     total = collect(1)
     token_grad[0] = total[:, :D].astype(BF)
-    tail = total[:, TB:]
-    weight_grad[0] = tail[:, OFF : OFF + TOP] + (
-        tail[:, OFF + TOP : OFF + 2 * TOP] + tail[:, OFF + 2 * TOP : OFF + 3 * TOP]
-    )
-    for copy in stores:
+    line = lax.broadcasted_iota(jnp.int32, (16, 128), 0)
+    spot = lax.broadcasted_iota(jnp.int32, (16, 128), 1) - OFF
+    chosen = (spot >= 0) & (spot < 3 * TOP) & (lax.rem(spot + 128, TOP) == line)
+    weight_grad[0] = contract(
+        chosen.astype(F32).astype(BF), total[:, TB:].astype(BF), 1, 1
+    )[:TOP]
+    for copy in saves:
         copy.wait()
     for copy in pending:
         copy.wait_send()
+
+
+def weight_kernel(
+    sizes,
+    rows_hbm,
+    grads_hbm,
+    hidden_hbm,
+    slope_gate_hbm,
+    slope_up_hbm,
+    mixed_in,
+    token_grad_in,
+    weight_grad_in,
+    mixed,
+    token_grad,
+    weight_grad,
+    gate_grad_hbm,
+    up_grad_hbm,
+    down_grad_hbm,
+    rows,
+    grads,
+    hidden,
+    slope_gate,
+    slope_up,
+    d_gate,
+    d_up,
+    d_down,
+    in_sem,
+    out_sem,
+):
+    D, DP, CAP, step = sizes
+    F = hidden.shape[1]
+    pairs = (
+        (rows_hbm, rows),
+        (slope_gate_hbm, slope_gate),
+        (slope_up_hbm, slope_up),
+        (grads_hbm, grads),
+        (hidden_hbm, hidden),
+    )
+    loads = [
+        pltpu.make_async_copy(source, target, in_sem.at[i])
+        for i, (source, target) in enumerate(pairs)
+    ]
+    for load in loads:
+        load.start()
+    mixed[...] = mixed_in[...]
+    token_grad[...] = token_grad_in[...]
+    weight_grad[...] = weight_grad_in[...]
+    stores = []
+
+    def fill(left, right, target, out, limit):
+        for low in range(0, limit, step):
+            size = min(step, limit - low)
+            target[low : low + size, :] = contract(
+                left(low, low + size), right[...], 0, 0
+            ).astype(BF)
+            copy = pltpu.make_async_copy(
+                target.at[pl.ds(low, size)],
+                out.at[0, pl.ds(low, size)],
+                out_sem.at[len(stores)],
+            )
+            copy.start()
+            stores.append(copy)
+
+    def row_columns(low, high):
+        return rows[:, :, low:high].reshape(2 * CAP, high - low)
+
+    loads[0].wait()
+    loads[1].wait()
+    fill(row_columns, slope_gate, d_gate, gate_grad_hbm, D)
+    loads[2].wait()
+    fill(row_columns, slope_up, d_up, up_grad_hbm, D)
+    loads[3].wait()
+    loads[4].wait()
+    fill(lambda low, high: hidden[:, low:high], grads, d_down, down_grad_hbm, F)
+    for copy in stores:
+        copy.wait()
 
 
 def local(tokens, experts, slots, route_weight, out_grad, w_gate, w_up, w_down):
@@ -397,25 +504,29 @@
     vmem = pl.BlockSpec(memory_space=pltpu.VMEM)
     anywhere = pl.BlockSpec(memory_space=pl.ANY)
     dma = pltpu.SemaphoreType.DMA
-    return pl.pallas_call(
+    by_choice = [jnp.swapaxes(a, 1, 2) for a in (experts, slots, route_weight)]
+    returned = (
+        jax.ShapeDtypeStruct((1, T, D), BF),
+        jax.ShapeDtypeStruct((1, T, D), BF),
+        jax.ShapeDtypeStruct((1, TOP, T), F32),
+    )
+    kept = (
+        jax.ShapeDtypeStruct((2, CAP, DP), BF),
+        jax.ShapeDtypeStruct((2 * CAP, D), BF),
+        jax.ShapeDtypeStruct((2 * CAP, F), BF),
+        jax.ShapeDtypeStruct((2 * CAP, F), BF),
+        jax.ShapeDtypeStruct((2 * CAP, F), BF),
+    )
+    results = pl.pallas_call(
         functools.partial(kernel, sizes),
-        out_shape=(
-            jax.ShapeDtypeStruct((1, T, D), BF),
-            jax.ShapeDtypeStruct((1, T, D), BF),
-            jax.ShapeDtypeStruct((1, T, TOP), F32),
-            jax.ShapeDtypeStruct((1, D, F), BF),
-            jax.ShapeDtypeStruct((1, D, F), BF),
-            jax.ShapeDtypeStruct((1, F, D), BF),
-        ),
+        out_shape=returned + kept,
         in_specs=[vmem] * 5 + [anywhere] * 3,
-        out_specs=[vmem] * 3 + [anywhere] * 3,
+        out_specs=[vmem] * 3 + [anywhere] * 5,
         scratch_shapes=[
             pltpu.VMEM((D, F), BF),
             pltpu.VMEM((D, F), BF),
             pltpu.VMEM((F, D), BF),
-            pltpu.VMEM((D, F), BF),
-            pltpu.VMEM((D, F), BF),
-            pltpu.VMEM((F, D), BF),
+            pltpu.VMEM((80, T), F32),
             pltpu.VMEM((2, S, T, DP), BF),
             pltpu.VMEM((2, NG, L, R, DP), BF),
             pltpu.VMEM((2, NG, L, R, DP), BF),
@@ -436,7 +547,7 @@
             pltpu.VMEM((2, CAP, D), F32),
             pltpu.VMEM((2, CAP, DP), BF),
             dma((3,)),
-            dma((3,)),
+            dma((5,)),
             dma((2, S)),
             dma((2, S)),
             dma((2, NG, L)),
@@ -445,17 +556,44 @@
             dma((2, NG, L)),
             dma((2, S)),
             dma((2, S)),
-            dma((4,)),
-            dma((4,)),
+            dma((6,)),
+            dma((6,)),
         ],
         compiler_params=pltpu.CompilerParams(
             collective_id=0, has_side_effects=True, vmem_limit_bytes=58 * 1024 * 1024
         ),
         cost_estimate=pl.CostEstimate(
-            flops=18 * 2 * CAP * D * F, bytes_accessed=12 * D * F, transcendentals=4 * CAP * F
+            flops=12 * 2 * CAP * D * F, bytes_accessed=6 * D * F, transcendentals=4 * CAP * F
         ),
         name="moe_layer",
-    )(tokens, experts, slots, route_weight, out_grad, w_gate, w_up, w_down)
+    )(tokens, *by_choice, out_grad, w_gate, w_up, w_down)
+    step = 512
+    copies = 2 * -(-D // step) + -(-F // step)
+    mixed, token_grad, weight_grad, gate_grad, up_grad, down_grad = pl.pallas_call(
+        functools.partial(weight_kernel, (D, DP, CAP, step)),
+        out_shape=returned
+        + (
+            jax.ShapeDtypeStruct((1, D, F), BF),
+            jax.ShapeDtypeStruct((1, D, F), BF),
+            jax.ShapeDtypeStruct((1, F, D), BF),
+        ),
+        in_specs=[anywhere] * 5 + [vmem] * 3,
+        out_specs=[vmem] * 3 + [anywhere] * 3,
+        scratch_shapes=[pltpu.VMEM(a.shape, a.dtype) for a in kept]
+        + [
+            pltpu.VMEM((D, F), BF),
+            pltpu.VMEM((D, F), BF),
+            pltpu.VMEM((F, D), BF),
+            dma((5,)),
+            dma((copies,)),
+        ],
+        compiler_params=pltpu.CompilerParams(vmem_limit_bytes=60 * 1024 * 1024),
+        cost_estimate=pl.CostEstimate(
+            flops=6 * 2 * CAP * D * F, bytes_accessed=6 * D * F, transcendentals=0
+        ),
+        name="weight_grads",
+    )(*results[3:], *results[:3])
+    return mixed, token_grad, jnp.swapaxes(weight_grad, 1, 2), gate_grad, up_grad, down_grad
 
 
 def solution(mesh):

time: 75.7 us -> 65.9 us (0.87)
  local copies, waits for them, and re-layouts: 15.6 us -> 0 us
  Pallas kernels: 59.1 us -> 65.1 us
    unnamed x12 -> x0, local copies, waits for them, and re-layouts: 14.2 us -> none
    pallas_call x1 -> x2, Pallas kernels: 59.1 us -> 65.1 us  [the longest x1 58.5 us: local(): pl.pallas_call(functools.partial(kernel, sizes), out_shape=returned + kep...]
    pallas_call x1 -> x0, local copies, waits for them, and re-layouts: 1.37 us -> none  [local(): pl.pallas_call(functools.partial(kernel, sizes), out_shape=(jax.ShapeDtyp...]
where the time goes in v2:
time: 65.9 us; the launch traced here: 65.7 us
  Pallas kernels  65.1 us (99%)
    pallas_call x1, Pallas kernels, local(): pl.pallas_call(functools.partial(kernel, sizes), out_shape=returned + kep...  58.5 us
    pallas_call x1, Pallas kernels, local(): pl.pallas_call(functools.partial(weight_kernel, (D, DP, CAP, step)), out_...  6.61 us

profile of v2, /device:TPU:0, one launch (start us, length us, event | category | flops | bytes accessed | tf_op | source)
XLA Modules:
  0.0 65.7 jit_solution(8923229276286303855)
XLA Ops:
  0.6 58.5 %moe_layer.1 = (bf16[1,32,1440]{2,1,0:T(8,128)(2,1)}, bf16[1,32,1440]{2,1,0:T(8,128)(2,1)}, f32[1,4,32]{2,1,0:T(4,128)}, bf16[2,128,1536]{2,1,0:T(8,128)(2,1)}, ...) custom-call(bf16[1,32,1440]{2,1,0:T(8,128)(2,1)} %tokens.1, ...), custom_call_target="tpu_custom_call" | custom-call | flops 3185049600 | bytes 6220800 | tf_op jit(solution)/shard_map/moe_layer/pallas_call | solution.py:520
  59.1 6.6 %weight_grads.1 = (bf16[1,32,1440]{2,1,0:T(8,128)(2,1)}, bf16[1,32,1440]{2,1,0:T(8,128)(2,1)}, f32[1,4,32]{2,1,0:T(4,128)}, bf16[1,1440,720]{2,1,0:T(8,128)(2,1)...) custom-call(bf16[2,128,1536]{2,1,0:T(8,128)(2,1)} %get-tuple-element.20.rows_hbm, ...), custom_call_target="tpu_custom_call" | custom-call | flops 1592524800 | bytes 6220800 | tf_op jit(solution)/shard_map/weight_grads/pallas_call | solution.py:572

commit v3 on v2

--- a/solution.py
+++ b/solution.py
@@ -55,6 +55,8 @@
     w_gate,
     w_up,
     w_down,
+    rows_t,
+    hidden_t,
     routing,
     gathered,
     plane_out,
@@ -284,17 +286,29 @@
         copy.start()
         saves.append(copy)
 
-    def await_plane(kind):
+    slot_lane = lax.broadcasted_iota(jnp.int32, (LR, CAP), 1).astype(F32) + 1.0
+
+    def compact(kind):
+        total = jnp.zeros((CAP, DP), F32)
         for jg in range(NG):
+            group = groups[jg]
             for j in range(1, L):
-                await_local(kind, plane_in, p_send, p_recv, groups[jg], j)
-
-    await_plane(0)
-    received = plane_in[0].reshape(NG * LR, DP)
-    slot_of = received[:, TB:].astype(F32)[:, OFF : OFF + 1]
-    slot_lane = lax.broadcasted_iota(jnp.int32, (NG * LR, CAP), 1).astype(F32) + 1.0
-    place[...] = (slot_of == slot_lane).astype(F32).astype(BF)
-    rows[0, r] = contract(place[...], received, 0, 0).astype(BF)
+                await_local(kind, plane_in, p_send, p_recv, group, j)
+            received = plane_in[kind, group].reshape(LR, DP)
+            if kind == 0:
+                slot_of = received[:, TB:].astype(F32)[:, OFF : OFF + 1]
+                place[group] = (slot_of == slot_lane).astype(F32).astype(BF)
+            total = total + contract(place[group], received, 0, 0)
+        rows[kind, r] = total.astype(BF)
+
+    def send_back(kind):
+        for jg in reversed(range(NG)):
+            group = groups[jg]
+            spread_rows = contract(place[group], reply[kind], 1, 0)
+            back_out[kind, group] = spread_rows.astype(BF).reshape(L, R, DP)
+            send_local(kind, back_out, back_in, r_send, r_recv, group)
+
+    compact(0)
     swap(0, rows.at[0, r], rows.at[0, r])
     for load in loads:
         load.wait()
@@ -306,8 +320,6 @@
     up = contract(x, w_up[...], 1, 0)
     up_pre[...] = up
     hidden[...] = ((up + 1.0) * gate * jax.nn.sigmoid(SWIGLU_ALPHA * gate)).astype(BF)
-    save(2, hidden, hidden_hbm)
-    save(0, rows.at[0], rows_hbm)
     for c, (low, high) in enumerate(halves):
         part = contract(hidden[...], w_down[:, low:high], 1, 0)
         partial[0, :, :, low:high] = part.reshape(2, CAP, high - low)
@@ -325,12 +337,9 @@
     out = partial[0, r] + other[0]
     reply[0, :, TB:] = jnp.zeros((CAP, 128), BF)
     reply[0, :, :D] = (weight_of(own_tail) * out).astype(BF)
-    back_out[0] = contract(place[...], reply[0], 1, 0).astype(BF).reshape(NG, L, R, DP)
-    for jg in reversed(range(NG)):
-        send_local(0, back_out, back_in, r_send, r_recv, groups[jg])
-
-    await_plane(1)
-    rows[1, r] = contract(place[...], plane_in[1].reshape(NG * LR, DP), 0, 0).astype(BF)
+    send_back(0)
+
+    compact(1)
     swap(1, rows.at[1, r], rows.at[1, r])
     own_grads = rows[1, r, :, :D].astype(F32)
     router_grad = jnp.sum(own_grads * out, axis=1, keepdims=True)
@@ -363,9 +372,7 @@
     reply[1, :, TB:] = jnp.where(
         slot_tail < 0.0, reply[1, :, TB:].astype(F32), reply_tail
     ).astype(BF)
-    back_out[1] = contract(place[...], reply[1], 1, 0).astype(BF).reshape(NG, L, R, DP)
-    for jg in reversed(range(NG)):
-        send_local(1, back_out, back_in, r_send, r_recv, groups[jg])
+    send_back(1)
 
     def send_home(kind):
         for jg in reversed(range(NG)):
@@ -387,6 +394,10 @@
                         (l, peer, r),
                     )
 
+    rows_t[...] = rows[0].reshape(2 * CAP, DP).T
+    save(0, rows_t, rows_hbm)
+    hidden_t[...] = hidden[...].T
+    save(2, hidden_t, hidden_hbm)
     send_home(0)
     send_home(1)
 
@@ -441,7 +452,7 @@
     out_sem,
 ):
     D, DP, CAP, step = sizes
-    F = hidden.shape[1]
+    F = hidden.shape[0]
     pairs = (
         (rows_hbm, rows),
         (slope_gate_hbm, slope_gate),
@@ -464,7 +475,7 @@
         for low in range(0, limit, step):
             size = min(step, limit - low)
             target[low : low + size, :] = contract(
-                left(low, low + size), right[...], 0, 0
+                left[low : low + size, :], right[...], 1, 0
             ).astype(BF)
             copy = pltpu.make_async_copy(
                 target.at[pl.ds(low, size)],
@@ -474,17 +485,14 @@
             copy.start()
             stores.append(copy)
 
-    def row_columns(low, high):
-        return rows[:, :, low:high].reshape(2 * CAP, high - low)
-
     loads[0].wait()
     loads[1].wait()
-    fill(row_columns, slope_gate, d_gate, gate_grad_hbm, D)
+    fill(rows, slope_gate, d_gate, gate_grad_hbm, D)
     loads[2].wait()
-    fill(row_columns, slope_up, d_up, up_grad_hbm, D)
+    fill(rows, slope_up, d_up, up_grad_hbm, D)
     loads[3].wait()
     loads[4].wait()
-    fill(lambda low, high: hidden[:, low:high], grads, d_down, down_grad_hbm, F)
+    fill(hidden, grads, d_down, down_grad_hbm, F)
     for copy in stores:
         copy.wait()
 
@@ -511,9 +519,9 @@
         jax.ShapeDtypeStruct((1, TOP, T), F32),
     )
     kept = (
-        jax.ShapeDtypeStruct((2, CAP, DP), BF),
+        jax.ShapeDtypeStruct((DP, 2 * CAP), BF),
         jax.ShapeDtypeStruct((2 * CAP, D), BF),
-        jax.ShapeDtypeStruct((2 * CAP, F), BF),
+        jax.ShapeDtypeStruct((F, 2 * CAP), BF),
         jax.ShapeDtypeStruct((2 * CAP, F), BF),
         jax.ShapeDtypeStruct((2 * CAP, F), BF),
     )
@@ -526,6 +534,8 @@
             pltpu.VMEM((D, F), BF),
             pltpu.VMEM((D, F), BF),
             pltpu.VMEM((F, D), BF),
+            pltpu.VMEM((DP, 2 * CAP), BF),
+            pltpu.VMEM((F, 2 * CAP), BF),
             pltpu.VMEM((80, T), F32),
             pltpu.VMEM((2, S, T, DP), BF),
             pltpu.VMEM((2, NG, L, R, DP), BF),
@@ -535,7 +545,7 @@
             pltpu.VMEM((2, S, T, DP), BF),
             pltpu.VMEM((2, S, T, DP), BF),
             pltpu.VMEM((NG, TT, LR), BF),
-            pltpu.VMEM((NG * LR, CAP), BF),
+            pltpu.VMEM((NG, LR, CAP), BF),
             pltpu.VMEM((2, 2, CAP, DP), BF),
             pltpu.VMEM((2 * CAP, D), BF),
             pltpu.VMEM((2 * CAP, F), BF),

time: 65.9 us -> 68 us (1.032)
  Pallas kernels: 65.1 us -> 67.1 us
    pallas_call x1, Pallas kernels: 58.5 us -> 60.6 us  [local(): pl.pallas_call(functools.partial(kernel, sizes), out_shape=returned + kep...]
where the time goes in v3:
time: 68 us; the launch traced here: 67.8 us
  Pallas kernels  67.1 us (99%)
    pallas_call x1, Pallas kernels, local(): pl.pallas_call(functools.partial(kernel, sizes), out_shape=returned + kep...  60.6 us
    pallas_call x1, Pallas kernels, local(): pl.pallas_call(functools.partial(weight_kernel, (D, DP, CAP, step)), out_...  6.5 us

profile of v3, /device:TPU:0, one launch (start us, length us, event | category | flops | bytes accessed | tf_op | source)
XLA Modules:
  0.0 67.8 jit_solution(2126682272684308949)
XLA Ops:
  0.6 60.6 %moe_layer.1 = (bf16[1,32,1440]{2,1,0:T(8,128)(2,1)}, bf16[1,32,1440]{2,1,0:T(8,128)(2,1)}, f32[1,4,32]{2,1,0:T(4,128)}, bf16[1536,256]{1,0:T(8,128)(2,1)}, bf16...) custom-call(bf16[1,32,1440]{2,1,0:T(8,128)(2,1)} %tokens.1, ...), custom_call_target="tpu_custom_call" | custom-call | flops 3185049600 | bytes 6220800 | tf_op jit(solution)/shard_map/moe_layer/pallas_call | solution.py:528
  61.3 6.5 %weight_grads.1 = (bf16[1,32,1440]{2,1,0:T(8,128)(2,1)}, bf16[1,32,1440]{2,1,0:T(8,128)(2,1)}, f32[1,4,32]{2,1,0:T(4,128)}, bf16[1,1440,720]{2,1,0:T(8,128)(2,1)...) custom-call(bf16[1536,256]{1,0:T(8,128)(2,1)} %get-tuple-element.20.rows_hbm, ...), custom_call_target="tpu_custom_call" | custom-call | flops 1592524800 | bytes 6220800 | tf_op jit(solution)/shard_map/weight_grads/pallas_call | solution.py:582

commit v4 on v2

--- a/solution.py
+++ b/solution.py
@@ -255,6 +255,13 @@
         copy = send(source, target, c_send.at[index], c_recv.at[index], (l, s, twin))
         return copy
 
+    def send_back(kind):
+        for jg in reversed(range(NG)):
+            group = groups[jg]
+            spread_rows = contract(place[pl.ds(group * LR, LR), :], reply[kind], 1, 0)
+            back_out[kind, group] = spread_rows.astype(BF).reshape(L, R, DP)
+            send_local(kind, back_out, back_in, r_send, r_recv, group)
+
     middle = -(-D // 256) * 128
     halves = ((0, middle), (middle, D))
 
@@ -325,9 +332,7 @@
     out = partial[0, r] + other[0]
     reply[0, :, TB:] = jnp.zeros((CAP, 128), BF)
     reply[0, :, :D] = (weight_of(own_tail) * out).astype(BF)
-    back_out[0] = contract(place[...], reply[0], 1, 0).astype(BF).reshape(NG, L, R, DP)
-    for jg in reversed(range(NG)):
-        send_local(0, back_out, back_in, r_send, r_recv, groups[jg])
+    send_back(0)
 
     await_plane(1)
     rows[1, r] = contract(place[...], plane_in[1].reshape(NG * LR, DP), 0, 0).astype(BF)
@@ -363,9 +368,7 @@
     reply[1, :, TB:] = jnp.where(
         slot_tail < 0.0, reply[1, :, TB:].astype(F32), reply_tail
     ).astype(BF)
-    back_out[1] = contract(place[...], reply[1], 1, 0).astype(BF).reshape(NG, L, R, DP)
-    for jg in reversed(range(NG)):
-        send_local(1, back_out, back_in, r_send, r_recv, groups[jg])
+    send_back(1)
 
     def send_home(kind):
         for jg in reversed(range(NG)):

time: 65.9 us -> 66.8 us (1.014)
  Pallas kernels: 65.1 us -> 65.9 us
    pallas_call x1, Pallas kernels: 58.5 us -> 59.3 us  [local(): pl.pallas_call(functools.partial(kernel, sizes), out_shape=returned + kep...]
where the time goes in v4:
time: 66.8 us; the launch traced here: 66.5 us
  Pallas kernels  65.9 us (99%)
    pallas_call x1, Pallas kernels, local(): pl.pallas_call(functools.partial(kernel, sizes), out_shape=returned + kep...  59.3 us
    pallas_call x1, Pallas kernels, local(): pl.pallas_call(functools.partial(weight_kernel, (D, DP, CAP, step)), out_...  6.6 us

profile of v4, /device:TPU:0, one launch (start us, length us, event | category | flops | bytes accessed | tf_op | source)
XLA Modules:
  0.0 66.5 jit_solution(3724274446456178367)
XLA Ops:
  0.6 59.3 %moe_layer.1 = (bf16[1,32,1440]{2,1,0:T(8,128)(2,1)}, bf16[1,32,1440]{2,1,0:T(8,128)(2,1)}, f32[1,4,32]{2,1,0:T(4,128)}, bf16[2,128,1536]{2,1,0:T(8,128)(2,1)}, ...) custom-call(bf16[1,32,1440]{2,1,0:T(8,128)(2,1)} %tokens.1, ...), custom_call_target="tpu_custom_call" | custom-call | flops 3185049600 | bytes 6220800 | tf_op jit(solution)/shard_map/moe_layer/pallas_call | solution.py:523
  59.9 6.6 %weight_grads.1 = (bf16[1,32,1440]{2,1,0:T(8,128)(2,1)}, bf16[1,32,1440]{2,1,0:T(8,128)(2,1)}, f32[1,4,32]{2,1,0:T(4,128)}, bf16[1,1440,720]{2,1,0:T(8,128)(2,1)...) custom-call(bf16[2,128,1536]{2,1,0:T(8,128)(2,1)} %get-tuple-element.20.rows_hbm, ...), custom_call_target="tpu_custom_call" | custom-call | flops 1592524800 | bytes 6220800 | tf_op jit(solution)/shard_map/weight_grads/pallas_call | solution.py:575
